TPU v7x, 512 devices: a whole 4x8x8 slice. The times are simulated.
512 devices in a mesh: chan: 16 (over x, y_hi, core), tm: 32 (over z, y_lo).
Axes of the slice: x: 4, y: 8 (y_hi: 2, y_lo: 4; y = y_hi * 4 + y_lo), z: 8, core: 2. Of those that a mesh axis runs over, the one named last changes fastest.
Arguments:
- traces: bfloat16 [16, 128, 128, 512], P('chan', 'tm'), may hold values from -6 to 6
- pair_listed: int32 [16, 8], P('chan'), may hold values from 0 to 1, as said below
- owner_slot: int32 [16, 8], P('chan'), may hold values from 0 to 31, as said below
- window_count: int32 [16, 8, 32], P('chan'), may hold values from 1 to 4, as said below
Outputs:
- stacks: float32 [16, 32, 128, 128], P('chan', 'tm')
Inputs may be any that keep to these rules, and one draw needn't show every extreme that they name: `pair_listed`: every distance is listed for block 0. `owner_slot`: distinct within each block's row. `window_count`: the windows entering are the first ones of the group; 4 is reached in every draw.
All inputs are finite; a program needn't handle non-finite values.
Results may differ from a plain program's by a relative error of at most 0.015.
Values may be sent and summed in bfloat16 or wider, within the bound.
No kernel may reach another device: no remote copies, remote signals or barrier semaphores. Data moves between devices by JAX's collectives and lax.ppermute only.
A program may use at most 64 MiB of HBM per device.

v0:
```python
import math
import jax
import jax.numpy as jnp
from jax import lax
from jax.sharding import PartitionSpec as P

BAND = 64
SMOOTH = 16
OFFSETS = 128
LAGS = 128
WATER = 0.1
PRECISE = lax.Precision.HIGHEST


def passed_along(block, axis, distance):
    devices = range(lax.axis_size(axis))
    route = [((i - distance) % len(devices), i) for i in devices]
    return lax.ppermute(block, axis, route)


def angles(left_index, right_index, period):
    product = left_index[:, None] * right_index[None, :] % period
    return 2.0 * math.pi / period * product.astype(jnp.float32)


def smooth_matrix():
    source = jnp.arange(BAND, dtype=jnp.int32)[:, None]
    target = jnp.arange(BAND, dtype=jnp.int32)[None, :]
    start = jnp.clip(target - SMOOTH // 2, 0, BAND - SMOOTH)
    inside = (source >= start) & (source < start + SMOOTH)
    return inside.astype(jnp.float32) / SMOOTH


def split_table(table):
    table_high = table.astype(jnp.bfloat16)
    table_low = (table - table_high.astype(jnp.float32)).astype(jnp.bfloat16)
    return (table_high, table_low)


def whiten(traces_local):
    windows, channels, samples = traces_local.shape
    flat_rows = traces_local.reshape(windows * channels, samples)
    phase_turn = angles(
        jnp.arange(samples, dtype=jnp.int32), jnp.arange(BAND, dtype=jnp.int32) + 1, samples
    )
    band_table = jnp.concatenate([jnp.cos(phase_turn), -jnp.sin(phase_turn)], axis=1)
    table_high, table_low = split_table(band_table)
    spectrum = jnp.dot(flat_rows, table_high, preferred_element_type=jnp.float32)
    spectrum = spectrum + jnp.dot(flat_rows, table_low, preferred_element_type=jnp.float32)
    real_part = spectrum[:, :BAND]
    imag_part = spectrum[:, BAND:]
    amplitude = jnp.sqrt(real_part * real_part + imag_part * imag_part)
    local_mean = jnp.dot(amplitude, smooth_matrix(), precision=PRECISE)
    water_level = local_mean + WATER * jnp.mean(amplitude, axis=1, keepdims=True) + 1e-06
    whitened = spectrum / jnp.concatenate([water_level, water_level], axis=1)
    return whitened.astype(jnp.bfloat16).reshape(windows, channels, 2 * BAND)


def channel_spectrum(block_data):
    channels = block_data.shape[1]
    padded = 2 * channels
    phase_turn = angles(
        jnp.arange(channels, dtype=jnp.int32), jnp.arange(padded, dtype=jnp.int32), padded
    )
    cos_high, cos_low = split_table(jnp.cos(phase_turn))
    sin_high, sin_low = split_table(jnp.sin(phase_turn))
    with_cos = jnp.einsum("wcg,ck->wkg", block_data, cos_high, preferred_element_type=jnp.float32)
    with_cos = with_cos + jnp.einsum(
        "wcg,ck->wkg", block_data, cos_low, preferred_element_type=jnp.float32
    )
    with_sin = jnp.einsum("wcg,ck->wkg", block_data, sin_high, preferred_element_type=jnp.float32)
    with_sin = with_sin + jnp.einsum(
        "wcg,ck->wkg", block_data, sin_low, preferred_element_type=jnp.float32
    )
    spec_real = with_cos[..., :BAND] + with_sin[..., BAND:]
    spec_imag = with_cos[..., BAND:] - with_sin[..., :BAND]
    return (spec_real, spec_imag)


def pair_term(arrived, own_real, own_imag, window_used, weight):
    src_real, src_imag = channel_spectrum(arrived)
    windows = arrived.shape[0]
    window_keep = (jnp.arange(windows, dtype=jnp.int32) < window_used).astype(jnp.float32)[
        :, None, None
    ]
    cross_real = jnp.sum(window_keep * (src_real * own_real + src_imag * own_imag), axis=0)
    cross_imag = jnp.sum(window_keep * (src_real * own_imag - src_imag * own_real), axis=0)
    padded = cross_real.shape[0]
    offset_steps = jnp.arange(OFFSETS, dtype=jnp.int32) - OFFSETS // 2
    phase_turn = angles(offset_steps, jnp.arange(padded, dtype=jnp.int32), padded)
    back_cos = jnp.cos(phase_turn) / padded
    back_sin = jnp.sin(phase_turn) / padded
    part_real = jnp.dot(back_cos, cross_real, precision=PRECISE) - jnp.dot(
        back_sin, cross_imag, precision=PRECISE
    )
    part_imag = jnp.dot(back_sin, cross_real, precision=PRECISE) + jnp.dot(
        back_cos, cross_imag, precision=PRECISE
    )
    return weight * jnp.concatenate([part_real, part_imag], axis=1)


def shards(traces, pair_listed, owner_slot, window_count):
    samples = traces.shape[3]
    whitened = whiten(traces[0])
    own_real, own_imag = channel_spectrum(whitened)
    pair_span = pair_listed.shape[1]
    groups = window_count.shape[2]
    group_index = lax.axis_index("tm")
    picked = jnp.arange(groups, dtype=jnp.int32) == group_index
    counts_here = jnp.sum(jnp.where(picked[None, :], window_count[0], 0), axis=1)
    totals = jnp.sum(window_count[0], axis=1).astype(jnp.float32)
    weights = pair_listed[0].astype(jnp.float32) / totals
    pair_terms = []
    moving = whitened
    for shift_step in range(pair_span):
        moving = passed_along(moving, "chan", 1)
        pair_terms.append(
            pair_term(moving, own_real, own_imag, counts_here[shift_step], weights[shift_step])
        )
    partials = jnp.stack(pair_terms)
    owners = owner_slot[0]
    summed = lax.psum(partials, "tm")
    owned_mask = (owners == group_index).astype(jnp.float32)
    owned = jnp.sum(owned_mask[:, None, None] * summed, axis=0)
    lag_angle = angles(
        jnp.arange(BAND, dtype=jnp.int32) + 1,
        jnp.arange(LAGS, dtype=jnp.int32) - LAGS // 2,
        samples,
    )
    lag_cos = jnp.cos(lag_angle)
    lag_sin = jnp.sin(lag_angle)
    stacked = jnp.dot(owned[:, :BAND], lag_cos, precision=PRECISE) - jnp.dot(
        owned[:, BAND:], lag_sin, precision=PRECISE
    )
    stacked = stacked / math.sqrt(BAND)
    return stacked[None, None]


def solution(mesh):
    placed = (P("chan", "tm", None, None), P("chan", None), P("chan", None), P("chan", None, None))
    return jax.shard_map(
        shards, mesh=mesh, in_specs=placed, out_specs=P("chan", "tm", None, None), check_vma=False
    )
```

profile of v0, /device:TPU:2, one launch (start us, length us, event | category | flops | bytes accessed | tf_op | source)
XLA Modules:
  0.0 484.5 jit_solution(13503771856990752241)
XLA Ops:
  6.6 1.1 fusion.35
  9.0 1.9 collective-permute-start
  17.3 1.2 compare_convert_fusion.1
  18.5 1.3 compare_convert_fusion.3
  24.0 7.8 %collective-permute-start.1 = (bf16[4,128,128]{1,2,0:T(8,128)(2,1)S(1)}, bf16[4,128,128]{1,2,0:T(8,128)(2,1)S(1)}, u32[]{:S(2)}, u32[]{:S(2)}) collective-permute-start(bf16[4,128,128]{1,2,0:T(8,128)(2,1)S(1)} %collective-permute-done), channel_id=1, source_target_pairs={{480,0},{0,32},{32,64},{64,96},{96,128},{128,160},{160,192},{192,2... | collective-permute-start | bytes 393224 | tf_op jit(solution)/shard_map/ppermute | solution.py:18
  31.9 3.3 collective-permute-done.1
  38.1 2.1 collective-permute-start.2
  40.2 8.9 %collective-permute-done.2 = bf16[4,128,128]{1,2,0:T(8,128)(2,1)S(1)} collective-permute-done((bf16[4,128,128]{1,2,0:T(8,128)(2,1)S(1)}, bf16[4,128,128]{1,2,0:T(8,128)(2,1)S(1)}, u32[]{:S(2)}, u32[]{:S(2)}) %collective-permute-start.2) | collective-permute-done | bytes 131104 | tf_op jit(solution)/shard_map/ppermute | solution.py:18
  52.0 1.9 collective-permute-start.3
  54.0 10.6 %collective-permute-done.3 = bf16[4,128,128]{1,2,0:T(8,128)(2,1)S(1)} collective-permute-done((bf16[4,128,128]{1,2,0:T(8,128)(2,1)S(1)}, bf16[4,128,128]{1,2,0:T(8,128)(2,1)S(1)}, u32[]{:S(2)}, u32[]{:S(2)}) %collective-permute-start.3) | collective-permute-done | bytes 131104 | tf_op jit(solution)/shard_map/ppermute | solution.py:18
  67.5 1.9 collective-permute-start.4
  69.5 9.2 %collective-permute-done.4 = bf16[4,128,128]{1,2,0:T(8,128)(2,1)S(1)} collective-permute-done((bf16[4,128,128]{1,2,0:T(8,128)(2,1)S(1)}, bf16[4,128,128]{1,2,0:T(8,128)(2,1)S(1)}, u32[]{:S(2)}, u32[]{:S(2)}) %collective-permute-start.4) | collective-permute-done | bytes 131104 | tf_op jit(solution)/shard_map/ppermute | solution.py:18
  81.6 1.9 collective-permute-start.5
  83.6 9.1 %collective-permute-done.5 = bf16[4,128,128]{1,2,0:T(8,128)(2,1)S(1)} collective-permute-done((bf16[4,128,128]{1,2,0:T(8,128)(2,1)S(1)}, bf16[4,128,128]{1,2,0:T(8,128)(2,1)S(1)}, u32[]{:S(2)}, u32[]{:S(2)}) %collective-permute-start.5) | collective-permute-done | bytes 131104 | tf_op jit(solution)/shard_map/ppermute | solution.py:18
  95.5 1.9 collective-permute-start.6
  97.5 9.1 %collective-permute-done.6 = bf16[4,128,128]{1,2,0:T(8,128)(2,1)S(1)} collective-permute-done((bf16[4,128,128]{1,2,0:T(8,128)(2,1)S(1)}, bf16[4,128,128]{1,2,0:T(8,128)(2,1)S(1)}, u32[]{:S(2)}, u32[]{:S(2)}) %collective-permute-start.6) | collective-permute-done | bytes 131104 | tf_op jit(solution)/shard_map/ppermute | solution.py:18
  109.5 2.3 collective-permute-start.7
  111.9 8.7 %collective-permute-done.7 = bf16[4,128,128]{1,2,0:T(8,128)(2,1)S(1)} collective-permute-done((bf16[4,128,128]{1,2,0:T(8,128)(2,1)S(1)}, bf16[4,128,128]{1,2,0:T(8,128)(2,1)S(1)}, u32[]{:S(2)}, u32[]{:S(2)}) %collective-permute-start.7) | collective-permute-done | bytes 131104 | tf_op jit(solution)/shard_map/ppermute | solution.py:18
  134.8 1.0 fusion.120
  138.3 0.8 fusion.7
  139.9 0.8 fusion.9
  157.4 317.5 %all-reduce.2.cloned.1.call-done = f32[8,128,128]{1,2,0:T(8,128)} async-done(((f32[8,128,128]{1,2,0:T(8,128)}), f32[8,128,128]{1,2,0:T(8,128)}) %all-reduce.2.cloned.1.call-update) | async-done | bytes 524304 | tf_op jit(solution)/shard_map/psum | solution.py:122
  474.9 1.2 multiply_reduce_fusion
  476.5 1.0 fusion.3
  (129 shorter events, 63.7 us)
Async XLA Ops:
  6.5 1.1 copy-start
  6.5 468.4 %all-reduce.2.cloned.1.call-start = ((), (), s32[]{:S(2)}) async-start(), calls=%async_computation | async-start | bytes 1048576 | tf_op jit(solution)/shard_map/psum | solution.py:122
  9.0 12.2 %collective-permute-start = (bf16[4,128,128]{1,2,0:T(8,128)(2,1)S(1)}, bf16[4,128,128]{1,2,0:T(8,128)(2,1)S(1)}, u32[]{:S(2)}, u32[]{:S(2)}) collective-permute-start(bf16[4,128,128]{1,2,0:T(8,128)(2,1)S(1)} %copy_bitcast_fusion), channel_id=1, source_target_pairs={{480,0},{0,32},{32,64},{64,96},{96,128},{128,160},{160,192},{192,2... | collective-permute-start | bytes 393224 | tf_op jit(solution)/shard_map/ppermute | solution.py:18
  13.7 0.7 copy-start.2
  18.5 1.3 copy-start.3
  24.0 11.2 %collective-permute-start.1 = (bf16[4,128,128]{1,2,0:T(8,128)(2,1)S(1)}, bf16[4,128,128]{1,2,0:T(8,128)(2,1)S(1)}, u32[]{:S(2)}, u32[]{:S(2)}) collective-permute-start(bf16[4,128,128]{1,2,0:T(8,128)(2,1)S(1)} %collective-permute-done), channel_id=1, source_target_pairs={{480,0},{0,32},{32,64},{64,96},{96,128},{128,160},{160,192},{192,2... | collective-permute-start | bytes 393224 | tf_op jit(solution)/shard_map/ppermute | solution.py:18
  38.1 11.1 %collective-permute-start.2 = (bf16[4,128,128]{1,2,0:T(8,128)(2,1)S(1)}, bf16[4,128,128]{1,2,0:T(8,128)(2,1)S(1)}, u32[]{:S(2)}, u32[]{:S(2)}) collective-permute-start(bf16[4,128,128]{1,2,0:T(8,128)(2,1)S(1)} %collective-permute-done.1), channel_id=1, source_target_pairs={{480,0},{0,32},{32,64},{64,96},{96,128},{128,160},{160,192},{192,2... | collective-permute-start | bytes 393224 | tf_op jit(solution)/shard_map/ppermute | solution.py:18
  52.0 12.6 %collective-permute-start.3 = (bf16[4,128,128]{1,2,0:T(8,128)(2,1)S(1)}, bf16[4,128,128]{1,2,0:T(8,128)(2,1)S(1)}, u32[]{:S(2)}, u32[]{:S(2)}) collective-permute-start(bf16[4,128,128]{1,2,0:T(8,128)(2,1)S(1)} %collective-permute-done.2), channel_id=1, source_target_pairs={{480,0},{0,32},{32,64},{64,96},{96,128},{128,160},{160,192},{192,2... | collective-permute-start | bytes 393224 | tf_op jit(solution)/shard_map/ppermute | solution.py:18
  67.5 11.2 %collective-permute-start.4 = (bf16[4,128,128]{1,2,0:T(8,128)(2,1)S(1)}, bf16[4,128,128]{1,2,0:T(8,128)(2,1)S(1)}, u32[]{:S(2)}, u32[]{:S(2)}) collective-permute-start(bf16[4,128,128]{1,2,0:T(8,128)(2,1)S(1)} %collective-permute-done.3), channel_id=1, source_target_pairs={{480,0},{0,32},{32,64},{64,96},{96,128},{128,160},{160,192},{192,2... | collective-permute-start | bytes 393224 | tf_op jit(solution)/shard_map/ppermute | solution.py:18
  81.6 11.1 %collective-permute-start.5 = (bf16[4,128,128]{1,2,0:T(8,128)(2,1)S(1)}, bf16[4,128,128]{1,2,0:T(8,128)(2,1)S(1)}, u32[]{:S(2)}, u32[]{:S(2)}) collective-permute-start(bf16[4,128,128]{1,2,0:T(8,128)(2,1)S(1)} %collective-permute-done.4), channel_id=1, source_target_pairs={{480,0},{0,32},{32,64},{64,96},{96,128},{128,160},{160,192},{192,2... | collective-permute-start | bytes 393224 | tf_op jit(solution)/shard_map/ppermute | solution.py:18
  95.5 11.1 %collective-permute-start.6 = (bf16[4,128,128]{1,2,0:T(8,128)(2,1)S(1)}, bf16[4,128,128]{1,2,0:T(8,128)(2,1)S(1)}, u32[]{:S(2)}, u32[]{:S(2)}) collective-permute-start(bf16[4,128,128]{1,2,0:T(8,128)(2,1)S(1)} %collective-permute-done.5), channel_id=1, source_target_pairs={{480,0},{0,32},{32,64},{64,96},{96,128},{128,160},{160,192},{192,2... | collective-permute-start | bytes 393224 | tf_op jit(solution)/shard_map/ppermute | solution.py:18
  109.5 11.1 %collective-permute-start.7 = (bf16[4,128,128]{1,2,0:T(8,128)(2,1)S(1)}, bf16[4,128,128]{1,2,0:T(8,128)(2,1)S(1)}, u32[]{:S(2)}, u32[]{:S(2)}) collective-permute-start(bf16[4,128,128]{1,2,0:T(8,128)(2,1)S(1)} %collective-permute-done.6), channel_id=1, source_target_pairs={{480,0},{0,32},{32,64},{64,96},{96,128},{128,160},{160,192},{192,2... | collective-permute-start | bytes 393224 | tf_op jit(solution)/shard_map/ppermute | solution.py:18
  156.6 0.8 copy-start.1
  156.6 0.8 copy-start.4
Sparse Core Ops, SparseCore 0:
  157.5 317.3 all-reduce.1
where the time goes:
time: 492 us; the launch traced here: 485 us
  waiting for transfers between devices  376 us (76%)
  matrix products  54 us (11%)
  starting transfers between devices  21.9 us (4%)
  other arithmetic  15.2 us (3%)
  between operations  14.3 us (3%)
    psum x1, waiting for transfers between devices, shards(): summed = lax.psum(partials, 'tm')  317 us
    ppermute x8, waiting for transfers between devices, passed_along(): return lax.ppermute(block, axis, route)  58.8 us
    unnamed x36, matrix products  24.8 us
    ppermute x8, starting transfers between devices, passed_along(): return lax.ppermute(block, axis, route)  21.9 us
  transfers between devices with their start and end apart: 9, of which 8 were waited for; matrix products, arithmetic and copies ran while one was open for 2% of the time, Pallas kernels for 0%

commit v1 on v0

--- a/solution.py
+++ b/solution.py
@@ -119,7 +119,7 @@
         )
     partials = jnp.stack(pair_terms)
     owners = owner_slot[0]
-    summed = lax.psum(partials, "tm")
+    summed = jnp.sum(lax.all_gather(partials, "tm"), axis=0)
     owned_mask = (owners == group_index).astype(jnp.float32)
     owned = jnp.sum(owned_mask[:, None, None] * summed, axis=0)
     lag_angle = angles(

time: 492 us -> 566 us (1.15)
  the two profiles are of different devices: /device:TPU:2 before, /device:TPU:1 now
where the time goes in v1:
time: 566 us; the launch traced here: 558 us
  waiting for transfers between devices  425 us (75%)
  matrix products  54.2 us (10%)
  starting transfers between devices  39.3 us (7%)
  other arithmetic  23.1 us (4%)
  between operations  14.3 us (3%)
    all_gather x1, waiting for transfers between devices, shards(): summed = jnp.sum(lax.all_gather(partials, 'tm'), axis=0)  378 us
    ppermute x8, waiting for transfers between devices, passed_along(): return lax.ppermute(block, axis, route)  46.8 us
    ppermute x8, starting transfers between devices, passed_along(): return lax.ppermute(block, axis, route)  39.3 us
    unnamed x36, matrix products  24.8 us
  transfers between devices with their start and end apart: 9, of which 8 were waited for; matrix products, arithmetic and copies ran while one was open for 2% of the time, Pallas kernels for 0%

profile of v1, /device:TPU:1, one launch (start us, length us, event | category | flops | bytes accessed | tf_op | source)
XLA Modules:
  0.0 558.2 jit_solution(3429657423931642067)
XLA Ops:
  6.6 1.1 fusion.35
  9.0 8.8 %collective-permute-start = (bf16[4,128,128]{1,2,0:T(8,128)(2,1)S(1)}, bf16[4,128,128]{1,2,0:T(8,128)(2,1)S(1)}, u32[]{:S(2)}, u32[]{:S(2)}) collective-permute-start(bf16[4,128,128]{1,2,0:T(8,128)(2,1)S(1)} %copy_bitcast_fusion), channel_id=1, source_target_pairs={{480,0},{0,32},{32,64},{64,96},{96,128},{128,160},{160,192},{192,2... | collective-permute-start | bytes 393224 | tf_op jit(solution)/shard_map/ppermute | solution.py:18
  25.5 1.2 compare_convert_fusion.1
  26.7 1.3 compare_convert_fusion.3
  32.3 1.9 collective-permute-start.1
  34.3 1.9 collective-permute-done.1
  39.0 8.5 %collective-permute-start.2 = (bf16[4,128,128]{1,2,0:T(8,128)(2,1)S(1)}, bf16[4,128,128]{1,2,0:T(8,128)(2,1)S(1)}, u32[]{:S(2)}, u32[]{:S(2)}) collective-permute-start(bf16[4,128,128]{1,2,0:T(8,128)(2,1)S(1)} %collective-permute-done.1), channel_id=1, source_target_pairs={{480,0},{0,32},{32,64},{64,96},{96,128},{128,160},{160,192},{192,2... | collective-permute-start | bytes 393224 | tf_op jit(solution)/shard_map/ppermute | solution.py:18
  47.6 2.5 collective-permute-done.2
  53.0 7.4 %collective-permute-start.3 = (bf16[4,128,128]{1,2,0:T(8,128)(2,1)S(1)}, bf16[4,128,128]{1,2,0:T(8,128)(2,1)S(1)}, u32[]{:S(2)}, u32[]{:S(2)}) collective-permute-start(bf16[4,128,128]{1,2,0:T(8,128)(2,1)S(1)} %collective-permute-done.2), channel_id=1, source_target_pairs={{480,0},{0,32},{32,64},{64,96},{96,128},{128,160},{160,192},{192,2... | collective-permute-start | bytes 393224 | tf_op jit(solution)/shard_map/ppermute | solution.py:18
  60.5 4.8 collective-permute-done.3
  68.2 5.3 collective-permute-start.4
  73.5 7.0 %collective-permute-done.4 = bf16[4,128,128]{1,2,0:T(8,128)(2,1)S(1)} collective-permute-done((bf16[4,128,128]{1,2,0:T(8,128)(2,1)S(1)}, bf16[4,128,128]{1,2,0:T(8,128)(2,1)S(1)}, u32[]{:S(2)}, u32[]{:S(2)}) %collective-permute-start.4) | collective-permute-done | bytes 131104 | tf_op jit(solution)/shard_map/ppermute | solution.py:18
  83.3 3.2 collective-permute-start.5
  86.6 9.1 %collective-permute-done.5 = bf16[4,128,128]{1,2,0:T(8,128)(2,1)S(1)} collective-permute-done((bf16[4,128,128]{1,2,0:T(8,128)(2,1)S(1)}, bf16[4,128,128]{1,2,0:T(8,128)(2,1)S(1)}, u32[]{:S(2)}, u32[]{:S(2)}) %collective-permute-start.5) | collective-permute-done | bytes 131104 | tf_op jit(solution)/shard_map/ppermute | solution.py:18
  98.5 1.9 collective-permute-start.6
  100.5 10.3 %collective-permute-done.6 = bf16[4,128,128]{1,2,0:T(8,128)(2,1)S(1)} collective-permute-done((bf16[4,128,128]{1,2,0:T(8,128)(2,1)S(1)}, bf16[4,128,128]{1,2,0:T(8,128)(2,1)S(1)}, u32[]{:S(2)}, u32[]{:S(2)}) %collective-permute-start.6) | collective-permute-done | bytes 131104 | tf_op jit(solution)/shard_map/ppermute | solution.py:18
  113.7 2.3 collective-permute-start.7
  116.1 11.3 %collective-permute-done.7 = bf16[4,128,128]{1,2,0:T(8,128)(2,1)S(1)} collective-permute-done((bf16[4,128,128]{1,2,0:T(8,128)(2,1)S(1)}, bf16[4,128,128]{1,2,0:T(8,128)(2,1)S(1)}, u32[]{:S(2)}, u32[]{:S(2)}) %collective-permute-start.7) | collective-permute-done | bytes 131104 | tf_op jit(solution)/shard_map/ppermute | solution.py:18
  141.4 1.0 fusion.126
  156.7 1.0 fusion.13
  163.6 1.0 copy.22
  164.6 377.8 %all-gather.3.cloned.1.call-done = f32[256,128,128]{2,1,0:T(8,128)} async-done(((f32[8,128,128]{2,1,0:T(8,128)}), f32[256,128,128]{2,1,0:T(8,128)}) %all-gather.3.cloned.1.call-update) | async-done | bytes 16777232 | tf_op jit(solution)/shard_map/all_gather | solution.py:122
  542.5 6.9 %reduce_sum.208 = f32[8,128,128]{2,1,0:T(8,128)S(1)} reduce(f32[32,8,128,128]{3,2,1,0:T(8,128)} %bitcast.292, f32[]{:T(128)} %constant.125.clone.1), dimensions={0}, to_apply=%region_19.20 | reduce | flops 4063232 | bytes 17301508 | tf_op jit(solution)/shard_map/reduce_sum | solution.py:122
  550.1 1.0 fusion.3
  (126 shorter events, 65.4 us)
Async XLA Ops:
  6.5 1.1 copy-start
  6.5 535.9 %all-gather.3.cloned.1.call-start = ((), (), s32[]{:S(2)}) async-start(), calls=%async_computation | async-start | bytes 17301504 | tf_op jit(solution)/shard_map/all_gather | solution.py:122
  9.0 20.4 %collective-permute-start = (bf16[4,128,128]{1,2,0:T(8,128)(2,1)S(1)}, bf16[4,128,128]{1,2,0:T(8,128)(2,1)S(1)}, u32[]{:S(2)}, u32[]{:S(2)}) collective-permute-start(bf16[4,128,128]{1,2,0:T(8,128)(2,1)S(1)} %copy_bitcast_fusion), channel_id=1, source_target_pairs={{480,0},{0,32},{32,64},{64,96},{96,128},{128,160},{160,192},{192,2... | collective-permute-start | bytes 393224 | tf_op jit(solution)/shard_map/ppermute | solution.py:18
  32.3 3.9 collective-permute-start.1
  39.0 11.1 %collective-permute-start.2 = (bf16[4,128,128]{1,2,0:T(8,128)(2,1)S(1)}, bf16[4,128,128]{1,2,0:T(8,128)(2,1)S(1)}, u32[]{:S(2)}, u32[]{:S(2)}) collective-permute-start(bf16[4,128,128]{1,2,0:T(8,128)(2,1)S(1)} %collective-permute-done.1), channel_id=1, source_target_pairs={{480,0},{0,32},{32,64},{64,96},{96,128},{128,160},{160,192},{192,2... | collective-permute-start | bytes 393224 | tf_op jit(solution)/shard_map/ppermute | solution.py:18
  53.0 12.3 %collective-permute-start.3 = (bf16[4,128,128]{1,2,0:T(8,128)(2,1)S(1)}, bf16[4,128,128]{1,2,0:T(8,128)(2,1)S(1)}, u32[]{:S(2)}, u32[]{:S(2)}) collective-permute-start(bf16[4,128,128]{1,2,0:T(8,128)(2,1)S(1)} %collective-permute-done.2), channel_id=1, source_target_pairs={{480,0},{0,32},{32,64},{64,96},{96,128},{128,160},{160,192},{192,2... | collective-permute-start | bytes 393224 | tf_op jit(solution)/shard_map/ppermute | solution.py:18
  68.2 12.3 %collective-permute-start.4 = (bf16[4,128,128]{1,2,0:T(8,128)(2,1)S(1)}, bf16[4,128,128]{1,2,0:T(8,128)(2,1)S(1)}, u32[]{:S(2)}, u32[]{:S(2)}) collective-permute-start(bf16[4,128,128]{1,2,0:T(8,128)(2,1)S(1)} %collective-permute-done.3), channel_id=1, source_target_pairs={{480,0},{0,32},{32,64},{64,96},{96,128},{128,160},{160,192},{192,2... | collective-permute-start | bytes 393224 | tf_op jit(solution)/shard_map/ppermute | solution.py:18
  83.3 12.3 %collective-permute-start.5 = (bf16[4,128,128]{1,2,0:T(8,128)(2,1)S(1)}, bf16[4,128,128]{1,2,0:T(8,128)(2,1)S(1)}, u32[]{:S(2)}, u32[]{:S(2)}) collective-permute-start(bf16[4,128,128]{1,2,0:T(8,128)(2,1)S(1)} %collective-permute-done.4), channel_id=1, source_target_pairs={{480,0},{0,32},{32,64},{64,96},{96,128},{128,160},{160,192},{192,2... | collective-permute-start | bytes 393224 | tf_op jit(solution)/shard_map/ppermute | solution.py:18
  98.5 12.3 %collective-permute-start.6 = (bf16[4,128,128]{1,2,0:T(8,128)(2,1)S(1)}, bf16[4,128,128]{1,2,0:T(8,128)(2,1)S(1)}, u32[]{:S(2)}, u32[]{:S(2)}) collective-permute-start(bf16[4,128,128]{1,2,0:T(8,128)(2,1)S(1)} %collective-permute-done.5), channel_id=1, source_target_pairs={{480,0},{0,32},{32,64},{64,96},{96,128},{128,160},{160,192},{192,2... | collective-permute-start | bytes 393224 | tf_op jit(solution)/shard_map/ppermute | solution.py:18
  113.7 13.7 %collective-permute-start.7 = (bf16[4,128,128]{1,2,0:T(8,128)(2,1)S(1)}, bf16[4,128,128]{1,2,0:T(8,128)(2,1)S(1)}, u32[]{:S(2)}, u32[]{:S(2)}) collective-permute-start(bf16[4,128,128]{1,2,0:T(8,128)(2,1)S(1)} %collective-permute-done.6), channel_id=1, source_target_pairs={{480,0},{0,32},{32,64},{64,96},{96,128},{128,160},{160,192},{192,2... | collective-permute-start | bytes 393224 | tf_op jit(solution)/shard_map/ppermute | solution.py:18
  130.3 34.3 %copy-start.1 = (s32[1,8]{1,0:T(1,128)S(1)}, s32[1,8]{1,0:T(1,128)}, u32[]{:S(2)}) copy-start(s32[1,8]{1,0:T(1,128)} %param.6) | copy-start | bytes 100
Sparse Core Ops, SparseCore 0:
  164.7 377.6 all-gather.2
